TPU v7x, 32 devices: a whole 2x2x4 slice. The times are simulated.
32 devices in a mesh: idx: 8 (over z, x), slab: 4 (over y, core).
Axes of the slice: x: 2, y: 2, z: 4, core: 2. Of those that a mesh axis runs over, the one named last changes fastest.
Arguments:
- amplitudes: bfloat16 [512, 2, 16384], P(('idx', 'slab')), may hold values from -6 to 6
- pair_irreps: int32 [512], replicated, may hold values from 0 to 7
- slab_irreps: int32 [2], replicated, may hold values from 0 to 7
- ladder_ints: bfloat16 [512, 512], P(None, 'slab'), may hold values from -0.75 to 0.75
- vv_blocks: bfloat16 [8, 128, 128], P(None, 'slab'), may hold values from -0.5 to 0.5
Outputs:
- residual: float32 [512, 2, 16384], P(('idx', 'slab'))
Inputs may be any that keep to these rules, and one draw needn't show every extreme that they name: `pair_irreps`: irrep labels. `slab_irreps`: irrep labels.
All inputs are finite; a program needn't handle non-finite values.
Results may differ from a plain program's by a relative error of at most 0.0055.
Values may be sent and summed in bfloat16 or wider, within the bound.
A program may use at most 128 MiB of HBM per device.

v0:
```python
import functools

import jax
import jax.numpy as jnp
from jax import lax
from jax.experimental import pallas as pl
from jax.experimental.pallas import tpu as pltpu
from jax.sharding import PartitionSpec as P

MESH = pl.DeviceIdType.MESH


def exchange_kernel(
    n_idx, n_slab, cw, t_ref, labels_ref, slab_labels_ref, row_ref, w_ref, v_ref, out_ref,
    recv, wfull, res, hole, vfull, rows_in, rows_out, labels, slab_labels,
    send1, recv1, send2, recv2, wsend, wrecv, vsend, vrecv, own_sems,
):
    n_dev = n_idx * n_slab
    pair_dev = t_ref.shape[1]
    square = t_ref.shape[2]
    width = t_ref.shape[0] * square // n_dev
    chunks = width // cw
    w_cols = w_ref.shape[1]
    v_rows = v_ref.shape[1]
    e = lax.axis_index("idx")
    s = lax.axis_index("slab")
    me = e * n_slab + s
    my_block = (s * n_idx + e) * pair_dev
    others = n_dev - 1

    def where(peer):
        return (peer // n_slab, peer % n_slab)

    barrier = pltpu.get_barrier_semaphore()

    def greet(j, carry):
        pl.semaphore_signal(barrier, inc=1, device_id=where((me + j) % n_dev), device_id_type=MESH)
        return carry

    lax.fori_loop(1, n_dev, greet, 0)
    pl.semaphore_wait(barrier, others)

    locals_ = [
        pltpu.make_async_copy(
            w_ref, wfull.at[:, pl.ds(pl.multiple_of(s * w_cols, 128), w_cols)], own_sems.at[0]
        ),
        pltpu.make_async_copy(
            v_ref, vfull.at[:, pl.ds(pl.multiple_of(s * v_rows, 16), v_rows), :], own_sems.at[1]
        ),
        pltpu.make_async_copy(labels_ref, labels, own_sems.at[2]),
        pltpu.make_async_copy(slab_labels_ref, slab_labels, own_sems.at[3]),
    ]
    for copy in locals_:
        copy.start()

    def order(j):
        return j

    def columns(device, k):
        first = device * width + k * cw
        return first // square, pl.ds(pl.multiple_of(first % square, 128), cw)

    def send_chunk(k):
        def body(j, carry):
            peer = (me + order(j)) % n_dev
            plane, place = columns(peer, k)
            pltpu.make_async_remote_copy(
                src_ref=t_ref.at[plane, :, place],
                dst_ref=recv.at[k, pl.ds(pl.multiple_of(my_block, 16), pair_dev), :],
                send_sem=send1,
                recv_sem=recv1.at[k],
                device_id=where(peer),
                device_id_type=MESH,
            ).start()
            return carry

        lax.fori_loop(1, n_dev, body, 0)
        plane, place = columns(me, k)
        recv[k, pl.ds(pl.multiple_of(my_block, 16), pair_dev), :] = t_ref[plane, :, place]

    def gather(j):
        peer = (s + j) % n_slab
        return (
            pltpu.make_async_remote_copy(
                src_ref=w_ref,
                dst_ref=wfull.at[:, pl.ds(pl.multiple_of(s * w_cols, 128), w_cols)],
                send_sem=wsend.at[j - 1],
                recv_sem=wrecv.at[j - 1],
                device_id=(e, peer),
                device_id_type=MESH,
            ),
            pltpu.make_async_remote_copy(
                src_ref=v_ref,
                dst_ref=vfull.at[:, pl.ds(pl.multiple_of(s * v_rows, 16), v_rows), :],
                send_sem=vsend.at[j - 1],
                recv_sem=vrecv.at[j - 1],
                device_id=(e, peer),
                device_id_type=MESH,
            ),
        )

    send_chunk(0)
    gathers = [gather(j) for j in range(1, n_slab)]
    for w_copy, v_copy in gathers:
        w_copy.start()
        v_copy.start()
    for k in range(1, chunks):
        send_chunk(k)
    for copy in locals_:
        copy.wait()
    for _, v_copy in gathers:
        v_copy.wait()

    side = vfull.shape[1]
    slabs = t_ref.shape[0]
    def particle(plane):

        def take(c, carry):
            rows_in[pl.ds(pl.multiple_of(c * pair_dev, 16), pair_dev), :] = t_ref[
                plane, :, pl.ds(pl.multiple_of(c * side, 128), side)
            ].astype(jnp.float32)
            return carry

        def one(i, carry):
            g = jnp.bitwise_xor(labels[me * pair_dev + i], slab_labels[plane])
            x = rows_in[pl.ds(i, side, stride=pair_dev), :].astype(jnp.bfloat16)
            rows_out[plane, pl.ds(i, side, stride=pair_dev), :] = jnp.dot(
                vfull[g], x, preferred_element_type=jnp.float32
            )
            return carry

        lax.fori_loop(0, side, take, 0, unroll=8)
        lax.fori_loop(0, pair_dev, one, 0, unroll=4)

    for plane in range(slabs):
        particle(plane)

    for w_copy, _ in gathers:
        w_copy.wait()

    pairs = recv.shape[1]
    tile = min(pairs, 512)
    irreps = vfull.shape[0]
    onehot = (
        row_ref[...] == lax.broadcasted_iota(jnp.int32, (irreps, pairs), 0)
    ).astype(jnp.float32).astype(jnp.bfloat16)

    def mask_columns(n, carry):
        cols = pl.ds(pl.multiple_of(n * tile, tile), tile)
        col = lax.broadcasted_iota(jnp.int32, (pairs, tile), 1) + n * tile
        row = lax.broadcasted_iota(jnp.int32, (pairs, tile), 0)
        p, q = col % pair_dev, col // pair_dev
        kl = ((q % n_idx) * n_slab + q // n_idx) * pair_dev + p
        moved = jnp.dot(
            onehot,
            (row == kl).astype(jnp.float32).astype(jnp.bfloat16),
            preferred_element_type=jnp.float32,
        ).astype(jnp.bfloat16)
        equal = lax.dot_general(
            onehot, moved, (((0,), (0,)), ((), ())), preferred_element_type=jnp.float32
        )
        wfull[:, cols] = jnp.where(
            equal > 0.5, wfull[:, cols].astype(jnp.float32), 0.0
        ).astype(jnp.bfloat16)
        return carry

    lax.fori_loop(0, pairs // tile, mask_columns, 0)

    for k in range(chunks):
        plane, place = columns(me, k)
        landed = recv.at[k, pl.ds(0, others * pair_dev), :]
        pltpu.make_async_copy(landed, landed, recv1.at[k]).wait()

        def multiply(m, carry):
            rows = pl.ds(pl.multiple_of(m * tile, tile), tile)
            res[k, rows, :] = jnp.dot(
                wfull[rows, :], recv[k], preferred_element_type=jnp.float32
            ).astype(jnp.bfloat16)
            return carry

        lax.fori_loop(0, pairs // tile, multiply, 0)

        def give(j, carry):
            peer = (me + order(j)) % n_dev
            pltpu.make_async_remote_copy(
                src_ref=res.at[k, pl.ds(pl.multiple_of(peer * pair_dev, 16), pair_dev), :],
                dst_ref=hole.at[plane, :, place],
                send_sem=send2,
                recv_sem=recv2.at[k],
                device_id=where(peer),
                device_id_type=MESH,
            ).start()
            return carry

        lax.fori_loop(1, n_dev, give, 0)
        hole[plane, :, place] = res[k, pl.ds(pl.multiple_of(me * pair_dev, 16), pair_dev), :]


    per_plane = n_dev // slabs
    for k in range(chunks):
        landed = recv.at[k, pl.ds(0, others * pair_dev), :]
        pltpu.make_async_copy(landed, landed, recv2.at[k]).wait()
        for plane in range(slabs):

            def finish(d, carry):
                for u in range(cw // side):
                    first = d * width + k * cw + u * side
                    cols = pl.ds(pl.multiple_of(first, 128), side)
                    rows = pl.ds(pl.multiple_of(first // side * pair_dev, 16), pair_dev)
                    out_ref[:, plane, cols] = rows_out[plane, rows, :] + hole[
                        plane, :, cols
                    ].astype(jnp.float32)
                return carry

            lax.fori_loop(0, per_plane, finish, 0, unroll=2)

    everything = recv.at[:, pl.ds(0, others * pair_dev), :]
    for sem in (send1, send2):
        pltpu.make_async_copy(everything, everything, sem).wait()


def ladder(t, pair_irreps, slab_irreps, w, v, n_idx, n_slab):
    slabs, pair_dev, square = t.shape
    n_dev = n_idx * n_slab
    pairs = w.shape[0]
    width = slabs * square // n_dev
    cw = min(width, 256)
    chunks = width // cw
    irreps, v_rows, side = v.shape
    block = (chunks, pairs, cw)
    vmem = pl.BlockSpec(memory_space=pltpu.VMEM)
    anywhere = pl.BlockSpec(memory_space=pl.ANY)
    held = 2 * (pairs * pairs + 12 * slabs * pair_dev * square)
    dma = pltpu.SemaphoreType.DMA
    return pl.pallas_call(
        functools.partial(exchange_kernel, n_idx, n_slab, cw),
        out_shape=jax.ShapeDtypeStruct((pair_dev, slabs, square), jnp.float32),
        in_specs=[vmem, anywhere, anywhere, vmem, anywhere, anywhere],
        out_specs=vmem,
        scratch_shapes=[
            pltpu.VMEM(block, jnp.bfloat16),
            pltpu.VMEM((pairs, pairs), jnp.bfloat16),
            pltpu.VMEM(block, jnp.bfloat16),
            pltpu.VMEM(t.shape, jnp.bfloat16),
            pltpu.VMEM((irreps, v_rows * n_slab, side), jnp.bfloat16),
            pltpu.VMEM((side * pair_dev, side), jnp.float32),
            pltpu.VMEM((slabs, side * pair_dev, side), jnp.float32),
            pltpu.SMEM(pair_irreps.shape, jnp.int32),
            pltpu.SMEM(slab_irreps.shape, jnp.int32),
            dma, dma((chunks,)), dma, dma((chunks,)),
            dma((n_slab - 1,)), dma((n_slab - 1,)), dma((n_slab - 1,)), dma((n_slab - 1,)), dma((4,)),
        ],
        compiler_params=pltpu.CompilerParams(
            collective_id=0, has_side_effects=True, vmem_limit_bytes=held + 10 * 2**20
        ),
        cost_estimate=pl.CostEstimate(
            flops=2 * pairs * pairs * width,
            bytes_accessed=8 * slabs * pair_dev * square,
            transcendentals=0,
        ),
    )(t, pair_irreps, slab_irreps, pair_irreps.reshape(1, pairs), w, v)


def body(amplitudes, pair_irreps, slab_irreps, ladder_ints, vv_blocks):
    n_idx = lax.axis_size("idx")
    n_slab = lax.axis_size("slab")
    t = amplitudes.transpose(1, 0, 2)
    out = ladder(t, pair_irreps, slab_irreps, ladder_ints, vv_blocks, n_idx, n_slab)
    return out


def solution(mesh):
    return jax.shard_map(
        body,
        mesh=mesh,
        in_specs=(P(("idx", "slab"), None, None), P(), P(), P(None, "slab"), P(None, "slab", None)),
        out_specs=P(("idx", "slab"), None, None),
        check_vma=False,
    )
```

profile of v0, /device:TPU:15, one launch (start us, length us, event | category | flops | bytes accessed | tf_op | source)
XLA Modules:
  0.0 56.1 jit_solution(12944470613957049951)
XLA Ops:
  0.0 0.0 copy-start.2
  0.0 0.0 copy-start.1
  0.0 0.0 copy-start
  0.0 0.0 copy-start.3
  0.0 1.8 %copy.8 = bf16[16,2,16384]{2,0,1:T(8,128)(2,1)S(1)} copy(bf16[16,2,16384]{2,1,0:T(2,128)(2,1)} %param.5) | data formatting | bytes 2097152 | tf_op args[0]
  1.9 0.0 copy-done.2
  1.9 0.0 copy-done.1
  1.9 0.0 copy-done
  1.9 0.0 copy-done.3
  1.9 52.9 %shard_map.55 = f32[16,2,16384]{2,1,0:T(2,128)S(1)} custom-call(bf16[2,16,16384]{2,1,0:T(8,128)(2,1)S(1)} %bitcast.4, s32[512]{0:T(512)S(1)} %copy-done.2, s32[2]{0:T(128)S(1)} %copy-done.3, s32[1,512]{1,0:T(1,128)S(1)} %bitcast.5, bf16[512,128]{1,0:T(8,128)(2,1)S(1)} %copy-done, bf16[8,32,128]{2,1,0:T(8,128)(2,1)S(1)} %copy-done.1), custom_call_target="tpu_custom_call" | custom-call | flops 536870912 | bytes 4194304 | tf_op jit(solution)/shard_map/pallas_call | solution.py:235
  54.8 1.3 %copy.10 = f32[16,2,16384]{2,1,0:T(2,128)} copy(f32[16,2,16384]{2,1,0:T(2,128)S(1)} %shard_map.55) | data formatting | bytes 4194304
Async XLA Ops:
  0.0 1.9 %copy-start.2 = (s32[512]{0:T(512)S(1)}, s32[512]{0:T(512)}, u32[]{:S(2)}) copy-start(s32[512]{0:T(512)} %labels_ref.1) | copy-start | bytes 6148
  0.0 1.9 %copy-start.1 = (bf16[8,32,128]{2,1,0:T(8,128)(2,1)S(1)}, bf16[8,32,128]{2,1,0:T(8,128)(2,1)}, u32[]{:S(2)}) copy-start(bf16[8,32,128]{2,1,0:T(8,128)(2,1)} %v_ref.1) | copy-start | bytes 196612
  0.0 1.9 %copy-start = (bf16[512,128]{1,0:T(8,128)(2,1)S(1)}, bf16[512,128]{1,0:T(8,128)(2,1)}, u32[]{:S(2)}) copy-start(bf16[512,128]{1,0:T(8,128)(2,1)} %w_ref.1) | copy-start | bytes 393220
  0.0 1.9 %copy-start.3 = (s32[2]{0:T(128)S(1)}, s32[2]{0:T(128)}, u32[]{:S(2)}) copy-start(s32[2]{0:T(128)} %slab_labels_ref.1) | copy-start | bytes 28
where the time goes:
time: 56.3 us; the launch traced here: 56.1 us
  Pallas kernels  52.9 us (94%)
  local copies, waits for them, and re-layouts  3.18 us (6%)
    pallas_call x1, Pallas kernels, ladder(): pl.pallas_call(functools.partial(exchange_kernel, n_idx, n_slab, cw), out...  52.9 us
    unnamed x10, local copies, waits for them, and re-layouts  3.18 us

commit v1 on v0

--- a/solution.py
+++ b/solution.py
@@ -219,7 +219,7 @@
         pltpu.make_async_copy(everything, everything, sem).wait()
 
 
-def ladder(t, pair_irreps, slab_irreps, w, v, n_idx, n_slab):
+def exchange(t, pair_irreps, slab_irreps, w, v, n_idx, n_slab):
     slabs, pair_dev, square = t.shape
     n_dev = n_idx * n_slab
     pairs = w.shape[0]
@@ -261,12 +261,285 @@
     )(t, pair_irreps, slab_irreps, pair_irreps.reshape(1, pairs), w, v)
 
 
+def ladder_kernel(
+    n_idx, n_slab, t_ref, labels_ref, slab_labels_ref, row_ref, w_ref, v_ref, out_ref,
+    recv, wfull, wide, res, hole, mine, vfull, vwide, row, labels, slab_labels,
+    send1, recv1, send2, recv2, wsend, wrecv, vsend, vrecv, own_sems, keep_sem,
+):
+    n_dev = n_idx * n_slab
+    pair_dev, side, slabs, _ = t_ref.shape
+    chunks = side // n_dev
+    pairs = recv.shape[1]
+    w_cols = w_ref.shape[1]
+    irreps, v_rows, _ = v_ref.shape
+    e = lax.axis_index("idx")
+    s = lax.axis_index("slab")
+    me = e * n_slab + s
+    my_block = (s * n_idx + e) * pair_dev
+    others = n_dev - 1
+
+    def where(peer):
+        return (peer // n_slab, peer % n_slab)
+
+    barrier = pltpu.get_barrier_semaphore()
+
+    def greet(j, carry):
+        pl.semaphore_signal(barrier, inc=1, device_id=where((me + j) % n_dev), device_id_type=MESH)
+        return carry
+
+    lax.fori_loop(1, n_dev, greet, 0)
+
+    keep = [
+        pltpu.make_async_copy(
+            t_ref.at[:, k * n_dev + me],
+            recv.at[k, pl.ds(pl.multiple_of(my_block, 16), pair_dev)],
+            keep_sem.at[k],
+        )
+        for k in range(chunks)
+    ]
+    locals_ = [
+        pltpu.make_async_copy(
+            w_ref, wfull.at[:, pl.ds(pl.multiple_of(s * w_cols, 128), w_cols)], own_sems.at[0]
+        ),
+        pltpu.make_async_copy(
+            v_ref, vfull.at[:, pl.ds(pl.multiple_of(s * v_rows, 16), v_rows), :], own_sems.at[1]
+        ),
+        pltpu.make_async_copy(labels_ref, labels, own_sems.at[2]),
+        pltpu.make_async_copy(slab_labels_ref, slab_labels, own_sems.at[3]),
+        pltpu.make_async_copy(row_ref, row, own_sems.at[4]),
+        pltpu.make_async_copy(t_ref, mine, own_sems.at[5]),
+    ]
+    for copy in keep + locals_:
+        copy.start()
+
+    pl.semaphore_wait(barrier, others)
+
+    def send_chunk(k):
+        def body(j, carry):
+            peer = (me + j) % n_dev
+            pltpu.make_async_remote_copy(
+                src_ref=t_ref.at[:, k * n_dev + peer],
+                dst_ref=recv.at[k, pl.ds(pl.multiple_of(my_block, 16), pair_dev)],
+                send_sem=send1,
+                recv_sem=recv1.at[k],
+                device_id=where(peer),
+                device_id_type=MESH,
+            ).start()
+            return carry
+
+        lax.fori_loop(1, n_dev, body, 0)
+
+    def gather(j):
+        peer = (s + j) % n_slab
+        return (
+            pltpu.make_async_remote_copy(
+                src_ref=w_ref,
+                dst_ref=wfull.at[:, pl.ds(pl.multiple_of(s * w_cols, 128), w_cols)],
+                send_sem=wsend.at[j - 1],
+                recv_sem=wrecv.at[j - 1],
+                device_id=(e, peer),
+                device_id_type=MESH,
+            ),
+            pltpu.make_async_remote_copy(
+                src_ref=v_ref,
+                dst_ref=vfull.at[:, pl.ds(pl.multiple_of(s * v_rows, 16), v_rows), :],
+                send_sem=vsend.at[j - 1],
+                recv_sem=vrecv.at[j - 1],
+                device_id=(e, peer),
+                device_id_type=MESH,
+            ),
+        )
+
+    send_chunk(0)
+    gathers = [gather(j) for j in range(1, n_slab)]
+    for w_copy, v_copy in gathers:
+        w_copy.start()
+        v_copy.start()
+    for k in range(1, chunks):
+        send_chunk(k)
+    for copy in locals_:
+        copy.wait()
+    for w_copy, _ in gathers:
+        w_copy.wait()
+
+    def equal(shape, left, right):
+        return (
+            left(lax.broadcasted_iota(jnp.int32, shape, 0))
+            == right(lax.broadcasted_iota(jnp.int32, shape, 1))
+        )
+
+    def ones(mask):
+        return mask.astype(jnp.float32).astype(jnp.bfloat16)
+
+    def same(x):
+        return x
+
+    def half(x):
+        return x // slabs
+
+    def rest(x):
+        return x % slabs
+
+    onehot = ones(row[...] == lax.broadcasted_iota(jnp.int32, (irreps, pairs), 0))
+
+    def column_pair(q):
+        p, q = q % pair_dev, q // pair_dev
+        return ((q % n_idx) * n_slab + q // n_idx) * pair_dev + p
+
+    moved = jnp.dot(
+        onehot, ones(equal((pairs, pairs), same, column_pair)), preferred_element_type=jnp.float32
+    ).astype(jnp.bfloat16)
+    allowed = lax.dot_general(
+        onehot, moved, (((0,), (0,)), ((), ())), preferred_element_type=jnp.float32
+    )
+    wfull[...] = jnp.where(allowed > 0.5, wfull[...].astype(jnp.float32), 0.0).astype(jnp.bfloat16)
+
+    tile = 256
+    spread = ones(equal((pairs, slabs * pairs), same, half))
+
+    def widen(m, carry):
+        down = ones(
+            equal((tile, tile // slabs), half, same)
+        )
+        part = jnp.dot(
+            down,
+            wfull[pl.ds(pl.multiple_of(m * (tile // slabs), 16), tile // slabs), :],
+            preferred_element_type=jnp.float32,
+        ).astype(jnp.bfloat16)
+        both = jnp.dot(part, spread, preferred_element_type=jnp.float32)
+        wide[pl.ds(pl.multiple_of(m * tile, 16), tile), :] = jnp.where(
+            equal(both.shape, rest, rest), both, 0.0
+        ).astype(jnp.bfloat16)
+        return carry
+
+    lax.fori_loop(0, slabs * pairs // tile, widen, 0)
+
+    for k in range(chunks):
+        keep[k].wait()
+        landed = recv.at[k, pl.ds(0, others * pair_dev)]
+        pltpu.make_async_copy(landed, landed, recv1.at[k]).wait()
+        right = recv[k].reshape(slabs * pairs, side)
+
+        for m in range(slabs * pairs // tile):
+            res[k, m * (tile // slabs) : (m + 1) * (tile // slabs)] = (
+                jnp.dot(wide[m * tile : (m + 1) * tile, :], right, preferred_element_type=jnp.float32)
+                .astype(jnp.bfloat16)
+                .reshape(tile // slabs, slabs, side)
+            )
+
+        def give(j, carry):
+            peer = (me + j) % n_dev
+            pltpu.make_async_remote_copy(
+                src_ref=res.at[k, pl.ds(pl.multiple_of(peer * pair_dev, 16), pair_dev)],
+                dst_ref=hole.at[:, k * n_dev + me],
+                send_sem=send2,
+                recv_sem=recv2.at[k],
+                device_id=where(peer),
+                device_id_type=MESH,
+            ).start()
+            return carry
+
+        lax.fori_loop(1, n_dev, give, 0)
+        hole[:, k * n_dev + me] = res[k, pl.ds(pl.multiple_of(me * pair_dev, 16), pair_dev)]
+
+    for _, v_copy in gathers:
+        v_copy.wait()
+
+    rows = slabs * side
+    for g in range(irreps):
+        tall = jnp.dot(
+            ones(equal((rows, side), half, same)), vfull[g], preferred_element_type=jnp.float32
+        ).astype(jnp.bfloat16)
+        both = jnp.dot(
+            tall, ones(equal((side, rows), same, half)), preferred_element_type=jnp.float32
+        )
+        together = equal((rows, rows), rest, rest)
+        for plane in range(slabs):
+            mask = together & (lax.broadcasted_iota(jnp.int32, (rows, rows), 0) % slabs == plane)
+            vwide[plane, g] = jnp.where(mask, both, 0.0).astype(jnp.bfloat16)
+
+    def particle(i, carry):
+        x = mine[i].reshape(rows, side)
+        total = jnp.zeros((rows, side), jnp.float32)
+        for plane in range(slabs):
+            g = jnp.bitwise_xor(labels[me * pair_dev + i], slab_labels[plane])
+            total += jnp.dot(vwide[plane, g], x, preferred_element_type=jnp.float32)
+        out_ref[i] = total
+        return carry
+
+    lax.fori_loop(0, pair_dev, particle, 0)
+
+    for k in range(chunks):
+        landed = recv.at[k, pl.ds(0, others * pair_dev)]
+        pltpu.make_async_copy(landed, landed, recv2.at[k]).wait()
+
+        def finish(i, carry):
+            place = slice(k * n_dev * slabs, (k + 1) * n_dev * slabs)
+            out_ref[i, place, :] += (
+                hole[i, k * n_dev : (k + 1) * n_dev]
+                .reshape(n_dev * slabs, side)
+                .astype(jnp.float32)
+            )
+            return carry
+
+        lax.fori_loop(0, pair_dev, finish, 0, unroll=4)
+
+    everything = recv.at[:, pl.ds(0, others * pair_dev)]
+    for sem in (send1, send2):
+        pltpu.make_async_copy(everything, everything, sem).wait()
+
+
+def ladder(amplitudes, pair_irreps, slab_irreps, w, v, n_idx, n_slab):
+    pair_dev, slabs, square = amplitudes.shape
+    n_dev = n_idx * n_slab
+    pairs = w.shape[0]
+    irreps, v_rows, side = v.shape
+    chunks = side // n_dev
+    t = amplitudes.reshape(pair_dev, slabs, side, side).transpose(0, 2, 1, 3)
+    operands = (t, pair_irreps, slab_irreps, pair_irreps.reshape(1, pairs), w, v)
+    hbm = pl.BlockSpec(memory_space=pltpu.HBM)
+    dma = pltpu.SemaphoreType.DMA
+    bf16 = jnp.bfloat16
+    out = pl.pallas_call(
+        functools.partial(ladder_kernel, n_idx, n_slab),
+        out_shape=jax.ShapeDtypeStruct((pair_dev, side * slabs, side), jnp.float32),
+        in_specs=[hbm] * 6,
+        out_specs=pl.BlockSpec(memory_space=pltpu.VMEM),
+        scratch_shapes=[
+            pltpu.VMEM((chunks, pairs, slabs, side), bf16),
+            pltpu.VMEM((pairs, pairs), bf16),
+            pltpu.VMEM((slabs * pairs, slabs * pairs), bf16),
+            pltpu.VMEM((chunks, pairs, slabs, side), bf16),
+            pltpu.VMEM(t.shape, bf16),
+            pltpu.VMEM(t.shape, bf16),
+            pltpu.VMEM((irreps, side, side), bf16),
+            pltpu.VMEM((slabs, irreps, slabs * side, slabs * side), bf16),
+            pltpu.VMEM((1, pairs), jnp.int32),
+            pltpu.SMEM(pair_irreps.shape, jnp.int32),
+            pltpu.SMEM(slab_irreps.shape, jnp.int32),
+            dma, dma((chunks,)), dma, dma((chunks,)),
+            dma((n_slab - 1,)), dma((n_slab - 1,)), dma((n_slab - 1,)), dma((n_slab - 1,)),
+            dma((6,)), dma((chunks,)),
+        ],
+        compiler_params=pltpu.CompilerParams(
+            collective_id=0, has_side_effects=True, vmem_limit_bytes=40 * 2**20
+        ),
+        cost_estimate=pl.CostEstimate(
+            flops=4 * pairs * pairs * slabs * square // n_dev,
+            bytes_accessed=8 * slabs * pair_dev * square,
+            transcendentals=0,
+        ),
+    )(*(pltpu.with_memory_space_constraint(x, pltpu.HBM) for x in operands))
+    return out.reshape(pair_dev, side, slabs, side).transpose(0, 2, 1, 3).reshape(amplitudes.shape)
+
+
 def body(amplitudes, pair_irreps, slab_irreps, ladder_ints, vv_blocks):
     n_idx = lax.axis_size("idx")
     n_slab = lax.axis_size("slab")
-    t = amplitudes.transpose(1, 0, 2)
-    out = ladder(t, pair_irreps, slab_irreps, ladder_ints, vv_blocks, n_idx, n_slab)
-    return out
+    whole = (amplitudes, pair_irreps, slab_irreps, ladder_ints, vv_blocks, n_idx, n_slab)
+    if vv_blocks.shape[2] % (n_idx * n_slab) == 0:
+        return ladder(*whole)
+    return exchange(amplitudes.transpose(1, 0, 2), *whole[1:])
 
 
 def solution(mesh):

time: 56.3 us -> 53.6 us (0.952)
  local copies, waits for them, and re-layouts: 3.18 us -> 1.32 us
  Pallas kernels: 52.9 us -> 52.1 us
    unnamed x10 -> x1, local copies, waits for them, and re-layouts: 3.18 us -> 1.32 us
    pallas_call x1, Pallas kernels: 52.9 us -> 52.1 us  [ladder(): pl.pallas_call(functools.partial(ladder_kernel, n_idx, n_slab), out_shape...]
where the time goes in v1:
time: 53.6 us; the launch traced here: 53.4 us
  Pallas kernels  52.1 us (97%)
  local copies, waits for them, and re-layouts  1.32 us (2%)
    pallas_call x1, Pallas kernels, ladder(): pl.pallas_call(functools.partial(ladder_kernel, n_idx, n_slab), out_shape...  52.1 us
    unnamed x1, local copies, waits for them, and re-layouts  1.32 us

profile of v1, /device:TPU:15, one launch (start us, length us, event | category | flops | bytes accessed | tf_op | source)
XLA Modules:
  0.0 53.4 jit_solution(2025288249647821248)
XLA Ops:
  0.0 52.1 %shard_map.55 = f32[16,256,128]{2,1,0:T(8,128)S(1)} custom-call(bf16[16,128,2,128]{3,2,1,0:T(2,128)(2,1)} %bitcast.10, s32[512]{0:T(512)} %labels_ref.1, s32[2]{0:T(128)} %slab_labels_ref.1, s32[1,512]{1,0:T(1,128)} %bitcast.11, bf16[512,128]{1,0:T(8,128)(2,1)} %w_ref.1, bf16[8,32,128]{2,1,0:T(8,128)(2,1)} %v_ref.1), custom_call_target="tpu_custom_call" | custom-call | flops 1073741824 | bytes 4194304 | tf_op jit(solution)/shard_map/pallas_call | solution.py:503
  52.1 1.3 %copy.8 = f32[16,2,16384]{2,1,0:T(2,128)} copy(f32[16,2,16384]{2,1,0:T(2,128)S(1)} %bitcast.9) | data formatting | bytes 4194304

commit v2 on v1

--- a/solution.py
+++ b/solution.py
@@ -264,34 +264,53 @@
 def ladder_kernel(
     n_idx, n_slab, t_ref, labels_ref, slab_labels_ref, row_ref, w_ref, v_ref, out_ref,
     recv, wfull, wide, res, hole, mine, vfull, vwide, row, labels, slab_labels,
-    send1, recv1, send2, recv2, wsend, wrecv, vsend, vrecv, own_sems, keep_sem,
+    send1, recv1, send2, recv2, wsend, wrecv, vsend, vrecv, own_sems, keep_sem, late,
 ):
     n_dev = n_idx * n_slab
     pair_dev, side, slabs, _ = t_ref.shape
-    chunks = side // n_dev
-    pairs = recv.shape[1]
+    chunks, pairs, width = recv.shape[:3]
     w_cols = w_ref.shape[1]
     irreps, v_rows, _ = v_ref.shape
     e = lax.axis_index("idx")
     s = lax.axis_index("slab")
+    z, x, y, core = e // 2, e % 2, s // 2, s % 2
     me = e * n_slab + s
     my_block = (s * n_idx + e) * pair_dev
     others = n_dev - 1
-
-    def where(peer):
-        return (peer // n_slab, peer % n_slab)
-
-    barrier = pltpu.get_barrier_semaphore()
-
-    def greet(j, carry):
-        pl.semaphore_signal(barrier, inc=1, device_id=where((me + j) % n_dev), device_id_type=MESH)
-        return carry
-
-    lax.fori_loop(1, n_dev, greet, 0)
+    plane_dev = n_dev // 4
+    group = 2 * plane_dev
+    inner = (z == 1) | (z == 2)
+    outer = (z == 0) | (z == 3)
+
+    def flip(bit, by):
+        return bit + by - 2 * bit * by
+
+    def partner(dz, q):
+        pz = flip(z // 2, dz // 2) * 2 + flip(z % 2, dz % 2)
+        return pz * 2 + flip(x, q // 4), flip(y, q // 2 % 2) * 2 + flip(core, q % 2)
+
+    def of_kind(i):
+        return partner(3 * (1 - i // plane_dev), plane_dev - 1 - i % plane_dev)
+
+    def of_other_kind(i):
+        return partner(2 - i // plane_dev, plane_dev - 1 - i % plane_dev)
+
+    def of_all(i):
+        return partner(3 - i // plane_dev, plane_dev - 1 - i % plane_dev)
+
+    def signal(sem, count, peer_of):
+        def body(i, carry):
+            pl.semaphore_signal(sem, inc=1, device_id=peer_of(i), device_id_type=MESH)
+            return carry
+
+        lax.fori_loop(0, count, body, 0)
+
+    def columns(k, device):
+        return pl.ds(k * n_dev * width + device * width, width)
 
     keep = [
         pltpu.make_async_copy(
-            t_ref.at[:, k * n_dev + me],
+            t_ref.at[:, columns(k, me)],
             recv.at[k, pl.ds(pl.multiple_of(my_block, 16), pair_dev)],
             keep_sem.at[k],
         )
@@ -309,25 +328,47 @@
         pltpu.make_async_copy(row_ref, row, own_sems.at[4]),
         pltpu.make_async_copy(t_ref, mine, own_sems.at[5]),
     ]
-    for copy in keep + locals_:
-        copy.start()
-
-    pl.semaphore_wait(barrier, others)
-
-    def send_chunk(k):
-        def body(j, carry):
-            peer = (me + j) % n_dev
+
+    def send(k, count, peer_of):
+        def body(i, carry):
+            pe, ps = peer_of(i)
             pltpu.make_async_remote_copy(
-                src_ref=t_ref.at[:, k * n_dev + peer],
+                src_ref=t_ref.at[:, columns(k, pe * n_slab + ps)],
                 dst_ref=recv.at[k, pl.ds(pl.multiple_of(my_block, 16), pair_dev)],
                 send_sem=send1,
                 recv_sem=recv1.at[k],
-                device_id=where(peer),
+                device_id=(pe, ps),
                 device_id_type=MESH,
             ).start()
             return carry
 
-        lax.fori_loop(1, n_dev, body, 0)
+        lax.fori_loop(0, count, body, 0)
+
+    barrier = pltpu.get_barrier_semaphore()
+    signal(barrier, group - 1, of_kind)
+
+    @pl.when(inner)
+    def _():
+        signal(barrier, group, of_other_kind)
+
+    for copy in keep + locals_:
+        copy.start()
+
+    @pl.when(inner)
+    def _():
+        pl.semaphore_wait(barrier, group - 1)
+        for k in range(chunks):
+            send(k, group - 1, of_kind)
+        pl.semaphore_wait(late, group)
+        for k in range(chunks):
+            send(k, group, of_other_kind)
+
+    @pl.when(outer)
+    def _():
+        pl.semaphore_wait(barrier, others)
+        signal(late, group, of_other_kind)
+        for k in range(chunks):
+            send(k, others, of_all)
 
     def gather(j):
         peer = (s + j) % n_slab
@@ -350,13 +391,10 @@
             ),
         )
 
-    send_chunk(0)
     gathers = [gather(j) for j in range(1, n_slab)]
     for w_copy, v_copy in gathers:
         w_copy.start()
         v_copy.start()
-    for k in range(1, chunks):
-        send_chunk(k)
     for copy in locals_:
         copy.wait()
     for w_copy, _ in gathers:
@@ -414,33 +452,49 @@
 
     lax.fori_loop(0, slabs * pairs // tile, widen, 0)
 
+    def give(k, far):
+        def body(j, carry):
+            t = j % 2
+            q = j // 2 - 2 * t
+            pe = (flip(z // 2, far) * 2 + t) * 2 + q // 4
+            ps = q // 2 % 2 * 2 + flip(core, q % 2)
+            peer = pe * n_slab + ps
+
+            @pl.when((q >= 0) & (q < plane_dev) & (peer != me))
+            def _():
+                pltpu.make_async_remote_copy(
+                    src_ref=res.at[k, pl.ds(pl.multiple_of(peer * pair_dev, 16), pair_dev)],
+                    dst_ref=hole.at[:, columns(k, me)],
+                    send_sem=send2,
+                    recv_sem=recv2.at[k],
+                    device_id=(pe, ps),
+                    device_id_type=MESH,
+                ).start()
+
+            return carry
+
+        lax.fori_loop(0, group + 4, body, 0)
+
     for k in range(chunks):
         keep[k].wait()
         landed = recv.at[k, pl.ds(0, others * pair_dev)]
         pltpu.make_async_copy(landed, landed, recv1.at[k]).wait()
-        right = recv[k].reshape(slabs * pairs, side)
+        right = jnp.concatenate(
+            [recv[k, :, u].reshape(slabs * pairs, side) for u in range(width)], axis=1
+        )
 
         for m in range(slabs * pairs // tile):
-            res[k, m * (tile // slabs) : (m + 1) * (tile // slabs)] = (
-                jnp.dot(wide[m * tile : (m + 1) * tile, :], right, preferred_element_type=jnp.float32)
-                .astype(jnp.bfloat16)
-                .reshape(tile // slabs, slabs, side)
-            )
-
-        def give(j, carry):
-            peer = (me + j) % n_dev
-            pltpu.make_async_remote_copy(
-                src_ref=res.at[k, pl.ds(pl.multiple_of(peer * pair_dev, 16), pair_dev)],
-                dst_ref=hole.at[:, k * n_dev + me],
-                send_sem=send2,
-                recv_sem=recv2.at[k],
-                device_id=where(peer),
-                device_id_type=MESH,
-            ).start()
-            return carry
-
-        lax.fori_loop(1, n_dev, give, 0)
-        hole[:, k * n_dev + me] = res[k, pl.ds(pl.multiple_of(me * pair_dev, 16), pair_dev)]
+            got = jnp.dot(
+                wide[m * tile : (m + 1) * tile, :], right, preferred_element_type=jnp.float32
+            ).astype(jnp.bfloat16)
+            for u in range(width):
+                res[k, m * (tile // slabs) : (m + 1) * (tile // slabs), u] = got[
+                    :, u * side : (u + 1) * side
+                ].reshape(tile // slabs, slabs, side)
+
+        give(k, 0)
+        give(k, 1)
+        hole[:, columns(k, me)] = res[k, pl.ds(pl.multiple_of(me * pair_dev, 16), pair_dev)]
 
     for _, v_copy in gathers:
         v_copy.wait()
@@ -474,11 +528,9 @@
         pltpu.make_async_copy(landed, landed, recv2.at[k]).wait()
 
         def finish(i, carry):
-            place = slice(k * n_dev * slabs, (k + 1) * n_dev * slabs)
-            out_ref[i, place, :] += (
-                hole[i, k * n_dev : (k + 1) * n_dev]
-                .reshape(n_dev * slabs, side)
-                .astype(jnp.float32)
+            part = side // chunks
+            out_ref[i, k * part * slabs : (k + 1) * part * slabs, :] += (
+                hole[i, k * part : (k + 1) * part].reshape(part * slabs, side).astype(jnp.float32)
             )
             return carry
 
@@ -494,7 +546,8 @@
     n_dev = n_idx * n_slab
     pairs = w.shape[0]
     irreps, v_rows, side = v.shape
-    chunks = side // n_dev
+    width = 2
+    chunks = side // n_dev // width
     t = amplitudes.reshape(pair_dev, slabs, side, side).transpose(0, 2, 1, 3)
     operands = (t, pair_irreps, slab_irreps, pair_irreps.reshape(1, pairs), w, v)
     hbm = pl.BlockSpec(memory_space=pltpu.HBM)
@@ -506,10 +559,10 @@
         in_specs=[hbm] * 6,
         out_specs=pl.BlockSpec(memory_space=pltpu.VMEM),
         scratch_shapes=[
-            pltpu.VMEM((chunks, pairs, slabs, side), bf16),
+            pltpu.VMEM((chunks, pairs, width, slabs, side), bf16),
             pltpu.VMEM((pairs, pairs), bf16),
             pltpu.VMEM((slabs * pairs, slabs * pairs), bf16),
-            pltpu.VMEM((chunks, pairs, slabs, side), bf16),
+            pltpu.VMEM((chunks, pairs, width, slabs, side), bf16),
             pltpu.VMEM(t.shape, bf16),
             pltpu.VMEM(t.shape, bf16),
             pltpu.VMEM((irreps, side, side), bf16),
@@ -519,7 +572,7 @@
             pltpu.SMEM(slab_irreps.shape, jnp.int32),
             dma, dma((chunks,)), dma, dma((chunks,)),
             dma((n_slab - 1,)), dma((n_slab - 1,)), dma((n_slab - 1,)), dma((n_slab - 1,)),
-            dma((6,)), dma((chunks,)),
+            dma((6,)), dma((chunks,)), pltpu.SemaphoreType.REGULAR,
         ],
         compiler_params=pltpu.CompilerParams(
             collective_id=0, has_side_effects=True, vmem_limit_bytes=40 * 2**20
@@ -537,7 +590,7 @@
     n_idx = lax.axis_size("idx")
     n_slab = lax.axis_size("slab")
     whole = (amplitudes, pair_irreps, slab_irreps, ladder_ints, vv_blocks, n_idx, n_slab)
-    if vv_blocks.shape[2] % (n_idx * n_slab) == 0:
+    if (n_idx, n_slab) == (8, 4):
         return ladder(*whole)
     return exchange(amplitudes.transpose(1, 0, 2), *whole[1:])
 

time: 53.6 us -> 54.6 us (1.019)
  Pallas kernels: 52.1 us -> 52.7 us
    pallas_call x1, Pallas kernels: 52.1 us -> 52.7 us  [ladder(): pl.pallas_call(functools.partial(ladder_kernel, n_idx, n_slab), out_shape...]
where the time goes in v2:
time: 54.6 us; the launch traced here: 54.1 us
  Pallas kernels  52.7 us (97%)
  local copies, waits for them, and re-layouts  1.32 us (2%)
    pallas_call x1, Pallas kernels, ladder(): pl.pallas_call(functools.partial(ladder_kernel, n_idx, n_slab), out_shape...  52.7 us
    unnamed x1, local copies, waits for them, and re-layouts  1.32 us

profile of v2, /device:TPU:15, one launch (start us, length us, event | category | flops | bytes accessed | tf_op | source)
XLA Modules:
  0.0 54.1 jit_solution(1202645146553196727)
XLA Ops:
  0.0 52.7 %shard_map.55 = f32[16,256,128]{2,1,0:T(8,128)S(1)} custom-call(bf16[16,128,2,128]{3,2,1,0:T(2,128)(2,1)} %bitcast.10, s32[512]{0:T(512)} %labels_ref.1, s32[2]{0:T(128)} %slab_labels_ref.1, s32[1,512]{1,0:T(1,128)} %bitcast.11, bf16[512,128]{1,0:T(8,128)(2,1)} %w_ref.1, bf16[8,32,128]{2,1,0:T(8,128)(2,1)} %v_ref.1), custom_call_target="tpu_custom_call" | custom-call | flops 1073741824 | bytes 4194304 | tf_op jit(solution)/shard_map/pallas_call | solution.py:556
  52.7 1.3 %copy.8 = f32[16,2,16384]{2,1,0:T(2,128)} copy(f32[16,2,16384]{2,1,0:T(2,128)S(1)} %bitcast.9) | data formatting | bytes 4194304

commit v3 on v2

--- a/solution.py
+++ b/solution.py
@@ -344,32 +344,6 @@
 
         lax.fori_loop(0, count, body, 0)
 
-    barrier = pltpu.get_barrier_semaphore()
-    signal(barrier, group - 1, of_kind)
-
-    @pl.when(inner)
-    def _():
-        signal(barrier, group, of_other_kind)
-
-    for copy in keep + locals_:
-        copy.start()
-
-    @pl.when(inner)
-    def _():
-        pl.semaphore_wait(barrier, group - 1)
-        for k in range(chunks):
-            send(k, group - 1, of_kind)
-        pl.semaphore_wait(late, group)
-        for k in range(chunks):
-            send(k, group, of_other_kind)
-
-    @pl.when(outer)
-    def _():
-        pl.semaphore_wait(barrier, others)
-        signal(late, group, of_other_kind)
-        for k in range(chunks):
-            send(k, others, of_all)
-
     def gather(j):
         peer = (s + j) % n_slab
         return (
@@ -392,9 +366,40 @@
         )
 
     gathers = [gather(j) for j in range(1, n_slab)]
-    for w_copy, v_copy in gathers:
-        w_copy.start()
-        v_copy.start()
+    def start_gathers():
+        for w_copy, v_copy in gathers:
+            w_copy.start()
+            v_copy.start()
+
+    barrier = pltpu.get_barrier_semaphore()
+    signal(barrier, group - 1, of_kind)
+
+    @pl.when(inner)
+    def _():
+        signal(barrier, group, of_other_kind)
+
+    for copy in keep + locals_:
+        copy.start()
+
+    @pl.when(inner)
+    def _():
+        pl.semaphore_wait(barrier, group - 1)
+        start_gathers()
+        send(0, group - 1, of_kind)
+        pl.semaphore_wait(late, group)
+        send(0, group, of_other_kind)
+        for k in range(1, chunks):
+            send(k, group - 1, of_kind)
+            send(k, group, of_other_kind)
+
+    @pl.when(outer)
+    def _():
+        pl.semaphore_wait(barrier, others)
+        signal(late, group, of_other_kind)
+        start_gathers()
+        for k in range(chunks):
+            send(k, others, of_all)
+
     for copy in locals_:
         copy.wait()
     for w_copy, _ in gathers:

time: 54.6 us -> 52.7 us (0.965)
  Pallas kernels: 52.7 us -> 50.9 us
    pallas_call x1, Pallas kernels: 52.7 us -> 50.9 us  [ladder(): pl.pallas_call(functools.partial(ladder_kernel, n_idx, n_slab), out_shape...]
where the time goes in v3:
time: 52.7 us; the launch traced here: 52.2 us
  Pallas kernels  50.9 us (97%)
  local copies, waits for them, and re-layouts  1.32 us (3%)
    pallas_call x1, Pallas kernels, ladder(): pl.pallas_call(functools.partial(ladder_kernel, n_idx, n_slab), out_shape...  50.9 us
    unnamed x1, local copies, waits for them, and re-layouts  1.32 us

profile of v3, /device:TPU:15, one launch (start us, length us, event | category | flops | bytes accessed | tf_op | source)
XLA Modules:
  0.0 52.2 jit_solution(13165721030131652418)
XLA Ops:
  0.0 50.9 %shard_map.55 = f32[16,256,128]{2,1,0:T(8,128)S(1)} custom-call(bf16[16,128,2,128]{3,2,1,0:T(2,128)(2,1)} %bitcast.10, s32[512]{0:T(512)} %labels_ref.1, s32[2]{0:T(128)} %slab_labels_ref.1, s32[1,512]{1,0:T(1,128)} %bitcast.11, bf16[512,128]{1,0:T(8,128)(2,1)} %w_ref.1, bf16[8,32,128]{2,1,0:T(8,128)(2,1)} %v_ref.1), custom_call_target="tpu_custom_call" | custom-call | flops 1073741824 | bytes 4194304 | tf_op jit(solution)/shard_map/pallas_call | solution.py:561
  50.9 1.3 %copy.8 = f32[16,2,16384]{2,1,0:T(2,128)} copy(f32[16,2,16384]{2,1,0:T(2,128)S(1)} %bitcast.9) | data formatting | bytes 4194304

commit v4 on v3

--- a/solution.py
+++ b/solution.py
@@ -264,7 +264,7 @@
 def ladder_kernel(
     n_idx, n_slab, t_ref, labels_ref, slab_labels_ref, row_ref, w_ref, v_ref, out_ref,
     recv, wfull, wide, res, hole, mine, vfull, vwide, row, labels, slab_labels,
-    send1, recv1, send2, recv2, wsend, wrecv, vsend, vrecv, own_sems, keep_sem, late,
+    send1, recv1, send2, recv2, wsend, wrecv, vsend, vrecv, own_sems, keep_sem, late, pre,
 ):
     n_dev = n_idx * n_slab
     pair_dev, side, slabs, _ = t_ref.shape
@@ -329,7 +329,7 @@
         pltpu.make_async_copy(t_ref, mine, own_sems.at[5]),
     ]
 
-    def send(k, count, peer_of):
+    def send(k, count, peer_of, first=0):
         def body(i, carry):
             pe, ps = peer_of(i)
             pltpu.make_async_remote_copy(
@@ -342,7 +342,7 @@
             ).start()
             return carry
 
-        lax.fori_loop(0, count, body, 0)
+        lax.fori_loop(first, count, body, 0)
 
     def gather(j):
         peer = (s + j) % n_slab
@@ -372,32 +372,79 @@
             v_copy.start()
 
     barrier = pltpu.get_barrier_semaphore()
-    signal(barrier, group - 1, of_kind)
+    def second_cores(i):
+        pe, ps = partner(3 * (i // 4), i % 4 * 2)
+        return pe, ps // 2 * 2 + 1
+
+    def facing(i):
+        return partner(3, i)
+
+    def mate(i):
+        return partner(0, 1)
 
     @pl.when(inner)
     def _():
+        signal(barrier, 2, facing)
+
+        def tell(i, carry):
+            pe, ps = second_cores(i)
+
+            @pl.when((pe % 2 != x) | (ps // 2 != y))
+            def _():
+                pl.semaphore_signal(barrier, inc=1, device_id=(pe, ps), device_id_type=MESH)
+
+            return carry
+
+        lax.fori_loop(0, plane_dev, tell, 0)
+        signal(barrier, 1, mate)
         signal(barrier, group, of_other_kind)
+
+    @pl.when(outer)
+    def _():
+        signal(barrier, group - 1, of_kind)
 
     for copy in keep + locals_:
         copy.start()
 
+    def send_facing():
+        for k in range(chunks):
+            send(k, plane_dev, of_kind, plane_dev - 2)
+
     @pl.when(inner)
     def _():
-        pl.semaphore_wait(barrier, group - 1)
+        @pl.when(core == 0)
+        def _():
+            pl.semaphore_wait(barrier, 3)
+            signal(pre, 1, mate)
+            send_facing()
+            pl.semaphore_wait(pre, 1)
+
+        @pl.when(core == 1)
+        def _():
+            pl.semaphore_wait(pre, 1)
+            send_facing()
+            pl.semaphore_wait(barrier, group - 1)
+            signal(pre, 1, mate)
+
+        send(0, plane_dev - 2, of_kind)
         start_gathers()
-        send(0, group - 1, of_kind)
+        send(0, group - 1, of_kind, plane_dev)
         pl.semaphore_wait(late, group)
         send(0, group, of_other_kind)
         for k in range(1, chunks):
-            send(k, group - 1, of_kind)
+            send(k, plane_dev - 2, of_kind)
+            send(k, group - 1, of_kind, plane_dev)
             send(k, group, of_other_kind)
 
     @pl.when(outer)
     def _():
         pl.semaphore_wait(barrier, others)
+        send(0, plane_dev, of_all)
         signal(late, group, of_other_kind)
+        send(0, group, of_all, plane_dev)
         start_gathers()
-        for k in range(chunks):
+        send(0, others, of_all, group)
+        for k in range(1, chunks):
             send(k, others, of_all)
 
     for copy in locals_:
@@ -460,7 +507,7 @@
     def give(k, far):
         def body(j, carry):
             t = j % 2
-            q = j // 2 - 2 * t
+            q = j // 2 - 4 * t
             pe = (flip(z // 2, far) * 2 + t) * 2 + q // 4
             ps = q // 2 % 2 * 2 + flip(core, q % 2)
             peer = pe * n_slab + ps
@@ -478,7 +525,7 @@
 
             return carry
 
-        lax.fori_loop(0, group + 4, body, 0)
+        lax.fori_loop(0, group + 8, body, 0)
 
     for k in range(chunks):
         keep[k].wait()
@@ -578,6 +625,7 @@
             dma, dma((chunks,)), dma, dma((chunks,)),
             dma((n_slab - 1,)), dma((n_slab - 1,)), dma((n_slab - 1,)), dma((n_slab - 1,)),
             dma((6,)), dma((chunks,)), pltpu.SemaphoreType.REGULAR,
+            pltpu.SemaphoreType.REGULAR,
         ],
         compiler_params=pltpu.CompilerParams(
             collective_id=0, has_side_effects=True, vmem_limit_bytes=40 * 2**20

time: 52.7 us -> 51.7 us (0.981)
  Pallas kernels: 50.9 us -> 49.9 us
    pallas_call x1, Pallas kernels: 50.9 us -> 49.9 us  [ladder(): pl.pallas_call(functools.partial(ladder_kernel, n_idx, n_slab), out_shape...]
where the time goes in v4:
time: 51.7 us; the launch traced here: 51.2 us
  Pallas kernels  49.9 us (97%)
  local copies, waits for them, and re-layouts  1.32 us (3%)
    pallas_call x1, Pallas kernels, ladder(): pl.pallas_call(functools.partial(ladder_kernel, n_idx, n_slab), out_shape...  49.9 us
    unnamed x1, local copies, waits for them, and re-layouts  1.32 us

profile of v4, /device:TPU:15, one launch (start us, length us, event | category | flops | bytes accessed | tf_op | source)
XLA Modules:
  0.0 51.2 jit_solution(7603732462764319151)
XLA Ops:
  0.0 49.9 %shard_map.55 = f32[16,256,128]{2,1,0:T(8,128)S(1)} custom-call(bf16[16,128,2,128]{3,2,1,0:T(2,128)(2,1)} %bitcast.10, s32[512]{0:T(512)} %labels_ref.1, s32[2]{0:T(128)} %slab_labels_ref.1, s32[1,512]{1,0:T(1,128)} %bitcast.11, bf16[512,128]{1,0:T(8,128)(2,1)} %w_ref.1, bf16[8,32,128]{2,1,0:T(8,128)(2,1)} %v_ref.1), custom_call_target="tpu_custom_call" | custom-call | flops 1073741824 | bytes 4194304 | tf_op jit(solution)/shard_map/pallas_call | solution.py:608
  49.9 1.3 %copy.8 = f32[16,2,16384]{2,1,0:T(2,128)} copy(f32[16,2,16384]{2,1,0:T(2,128)S(1)} %bitcast.9) | data formatting | bytes 4194304

commit v5 on v4

--- a/solution.py
+++ b/solution.py
@@ -507,9 +507,10 @@
     def give(k, far):
         def body(j, carry):
             t = j % 2
-            q = j // 2 - 4 * t
-            pe = (flip(z // 2, far) * 2 + t) * 2 + q // 4
-            ps = q // 2 % 2 * 2 + flip(core, q % 2)
+            q = j // 2 - 2 * t
+            right, up = q // 4, q // 2 % 2
+            pe = (flip(z // 2, far) * 2 + t) * 2 + right + t * (up - right)
+            ps = (up + t * (right - up)) * 2 + flip(core, q % 2)
             peer = pe * n_slab + ps
 
             @pl.when((q >= 0) & (q < plane_dev) & (peer != me))
@@ -544,8 +545,8 @@
                     :, u * side : (u + 1) * side
                 ].reshape(tile // slabs, slabs, side)
 
+        give(k, 1)
         give(k, 0)
-        give(k, 1)
         hole[:, columns(k, me)] = res[k, pl.ds(pl.multiple_of(me * pair_dev, 16), pair_dev)]
 
     for _, v_copy in gathers:

time: 51.7 us -> 51.4 us (level)
  no operation moved by 1% of the time
where the time goes in v5:
time: 51.4 us; the launch traced here: 51.2 us
  Pallas kernels  49.9 us (97%)
  local copies, waits for them, and re-layouts  1.32 us (3%)
    pallas_call x1, Pallas kernels, ladder(): pl.pallas_call(functools.partial(ladder_kernel, n_idx, n_slab), out_shape...  49.9 us
    unnamed x1, local copies, waits for them, and re-layouts  1.32 us

profile of v5, /device:TPU:15, one launch (start us, length us, event | category | flops | bytes accessed | tf_op | source)
XLA Modules:
  0.0 51.2 jit_solution(2955412970876106969)
XLA Ops:
  0.0 49.9 %shard_map.55 = f32[16,256,128]{2,1,0:T(8,128)S(1)} custom-call(bf16[16,128,2,128]{3,2,1,0:T(2,128)(2,1)} %bitcast.10, s32[512]{0:T(512)} %labels_ref.1, s32[2]{0:T(128)} %slab_labels_ref.1, s32[1,512]{1,0:T(1,128)} %bitcast.11, bf16[512,128]{1,0:T(8,128)(2,1)} %w_ref.1, bf16[8,32,128]{2,1,0:T(8,128)(2,1)} %v_ref.1), custom_call_target="tpu_custom_call" | custom-call | flops 1073741824 | bytes 4194304 | tf_op jit(solution)/shard_map/pallas_call | solution.py:609
  49.9 1.3 %copy.8 = f32[16,2,16384]{2,1,0:T(2,128)} copy(f32[16,2,16384]{2,1,0:T(2,128)S(1)} %bitcast.9) | data formatting | bytes 4194304

commit v6 on v5

--- a/solution.py
+++ b/solution.py
@@ -376,6 +376,14 @@
         pe, ps = partner(3 * (i // 4), i % 4 * 2)
         return pe, ps // 2 * 2 + 1
 
+    def other_second_cores(i):
+        pe, ps = partner(3 - 3 * (i // 4), (3 - i % 4) * 2)
+        return pe, ps // 2 * 2 + 1
+
+    def first_cores_of_other_kind(i):
+        pe, ps = partner(2 - i // 4, i % 4 * 2)
+        return pe, ps // 2 * 2
+
     def facing(i):
         return partner(3, i)
 
@@ -397,11 +405,12 @@
 
         lax.fori_loop(0, plane_dev, tell, 0)
         signal(barrier, 1, mate)
-        signal(barrier, group, of_other_kind)
+        signal(barrier, plane_dev, first_cores_of_other_kind)
 
     @pl.when(outer)
     def _():
-        signal(barrier, group - 1, of_kind)
+        signal(barrier, plane_dev - 1, other_second_cores)
+        signal(barrier, 1, mate)
 
     for copy in keep + locals_:
         copy.start()
@@ -429,21 +438,37 @@
         send(0, plane_dev - 2, of_kind)
         start_gathers()
         send(0, group - 1, of_kind, plane_dev)
-        pl.semaphore_wait(late, group)
+        pl.semaphore_wait(late, plane_dev)
         send(0, group, of_other_kind)
         for k in range(1, chunks):
             send(k, plane_dev - 2, of_kind)
             send(k, group - 1, of_kind, plane_dev)
             send(k, group, of_other_kind)
 
-    @pl.when(outer)
+    @pl.when(outer & (core == 0))
     def _():
-        pl.semaphore_wait(barrier, others)
-        send(0, plane_dev, of_all)
+        pl.semaphore_wait(barrier, group + 1)
+        signal(pre, 1, mate)
         signal(late, group, of_other_kind)
-        send(0, group, of_all, plane_dev)
+        send(0, plane_dev, of_other_kind)
+        pl.semaphore_wait(pre, 1)
+        send(0, plane_dev, of_kind)
         start_gathers()
-        send(0, others, of_all, group)
+        send(0, group, of_other_kind, plane_dev)
+        send(0, group - 1, of_kind, plane_dev)
+        for k in range(1, chunks):
+            send(k, others, of_all)
+
+    @pl.when(outer & (core == 1))
+    def _():
+        pl.semaphore_wait(barrier, group - 1)
+        signal(pre, 1, mate)
+        send(0, plane_dev, of_kind)
+        pl.semaphore_wait(pre, 1)
+        send(0, plane_dev, of_other_kind)
+        start_gathers()
+        send(0, group, of_other_kind, plane_dev)
+        send(0, group - 1, of_kind, plane_dev)
         for k in range(1, chunks):
             send(k, others, of_all)
 
@@ -519,7 +544,7 @@
                     src_ref=res.at[k, pl.ds(pl.multiple_of(peer * pair_dev, 16), pair_dev)],
                     dst_ref=hole.at[:, columns(k, me)],
                     send_sem=send2,
-                    recv_sem=recv2.at[k],
+                    recv_sem=recv2.at[4 * k + z],
                     device_id=(pe, ps),
                     device_id_type=MESH,
                 ).start()
@@ -576,18 +601,23 @@
 
     lax.fori_loop(0, pair_dev, particle, 0)
 
+    part = plane_dev * width
+    order = (z, z + 1 - 2 * (z % 2), 3 - 3 * (z // 2), 2 - z // 2)
     for k in range(chunks):
-        landed = recv.at[k, pl.ds(0, others * pair_dev)]
-        pltpu.make_async_copy(landed, landed, recv2.at[k]).wait()
-
-        def finish(i, carry):
-            part = side // chunks
-            out_ref[i, k * part * slabs : (k + 1) * part * slabs, :] += (
-                hole[i, k * part : (k + 1) * part].reshape(part * slabs, side).astype(jnp.float32)
-            )
-            return carry
-
-        lax.fori_loop(0, pair_dev, finish, 0, unroll=4)
+        for turn, plane in enumerate(order):
+            senders = plane_dev - 1 if turn == 0 else plane_dev
+            landed = recv.at[k, pl.ds(0, senders * pair_dev)]
+            pltpu.make_async_copy(landed, landed, recv2.at[4 * k + plane]).wait()
+            first = k * n_dev * width + plane * part
+
+            def finish(i, carry):
+                place = pl.ds(pl.multiple_of(first * slabs, 8), part * slabs)
+                out_ref[i, place, :] += (
+                    hole[i, pl.ds(first, part)].reshape(part * slabs, side).astype(jnp.float32)
+                )
+                return carry
+
+            lax.fori_loop(0, pair_dev, finish, 0, unroll=8)
 
     everything = recv.at[:, pl.ds(0, others * pair_dev)]
     for sem in (send1, send2):
@@ -623,7 +653,7 @@
             pltpu.VMEM((1, pairs), jnp.int32),
             pltpu.SMEM(pair_irreps.shape, jnp.int32),
             pltpu.SMEM(slab_irreps.shape, jnp.int32),
-            dma, dma((chunks,)), dma, dma((chunks,)),
+            dma, dma((chunks,)), dma, dma((4 * chunks,)),
             dma((n_slab - 1,)), dma((n_slab - 1,)), dma((n_slab - 1,)), dma((n_slab - 1,)),
             dma((6,)), dma((chunks,)), pltpu.SemaphoreType.REGULAR,
             pltpu.SemaphoreType.REGULAR,

time: 51.4 us -> 51 us (level)
  no operation moved by 1% of the time
where the time goes in v6:
time: 51 us; the launch traced here: 50.8 us
  Pallas kernels  49.5 us (97%)
  local copies, waits for them, and re-layouts  1.32 us (3%)
    pallas_call x1, Pallas kernels, ladder(): pl.pallas_call(functools.partial(ladder_kernel, n_idx, n_slab), out_shape...  49.5 us
    unnamed x1, local copies, waits for them, and re-layouts  1.32 us

profile of v6, /device:TPU:15, one launch (start us, length us, event | category | flops | bytes accessed | tf_op | source)
XLA Modules:
  0.0 50.8 jit_solution(6745987470986683284)
XLA Ops:
  0.0 49.5 %shard_map.55 = f32[16,256,128]{2,1,0:T(8,128)S(1)} custom-call(bf16[16,128,2,128]{3,2,1,0:T(2,128)(2,1)} %bitcast.10, s32[512]{0:T(512)} %labels_ref.1, s32[2]{0:T(128)} %slab_labels_ref.1, s32[1,512]{1,0:T(1,128)} %bitcast.11, bf16[512,128]{1,0:T(8,128)(2,1)} %w_ref.1, bf16[8,32,128]{2,1,0:T(8,128)(2,1)} %v_ref.1), custom_call_target="tpu_custom_call" | custom-call | flops 1073741824 | bytes 4194304 | tf_op jit(solution)/shard_map/pallas_call | solution.py:639
  49.5 1.3 %copy.8 = f32[16,2,16384]{2,1,0:T(2,128)} copy(f32[16,2,16384]{2,1,0:T(2,128)S(1)} %bitcast.9) | data formatting | bytes 4194304

commit v7 on v6

--- a/solution.py
+++ b/solution.py
@@ -570,8 +570,8 @@
                     :, u * side : (u + 1) * side
                 ].reshape(tile // slabs, slabs, side)
 
-        give(k, 1)
-        give(k, 0)
+        give(k, k)
+        give(k, 1 - k)
         hole[:, columns(k, me)] = res[k, pl.ds(pl.multiple_of(me * pair_dev, 16), pair_dev)]
 
     for _, v_copy in gathers:

time: 51 us -> 51.1 us (level)
  no operation moved by 1% of the time
where the time goes in v7:
time: 51.1 us; the launch traced here: 50.8 us
  Pallas kernels  49.5 us (97%)
  local copies, waits for them, and re-layouts  1.32 us (3%)
    pallas_call x1, Pallas kernels, ladder(): pl.pallas_call(functools.partial(ladder_kernel, n_idx, n_slab), out_shape...  49.5 us
    unnamed x1, local copies, waits for them, and re-layouts  1.32 us

profile of v7, /device:TPU:15, one launch (start us, length us, event | category | flops | bytes accessed | tf_op | source)
XLA Modules:
  0.0 50.8 jit_solution(11498553812780148615)
XLA Ops:
  0.0 49.5 %shard_map.55 = f32[16,256,128]{2,1,0:T(8,128)S(1)} custom-call(bf16[16,128,2,128]{3,2,1,0:T(2,128)(2,1)} %bitcast.10, s32[512]{0:T(512)} %labels_ref.1, s32[2]{0:T(128)} %slab_labels_ref.1, s32[1,512]{1,0:T(1,128)} %bitcast.11, bf16[512,128]{1,0:T(8,128)(2,1)} %w_ref.1, bf16[8,32,128]{2,1,0:T(8,128)(2,1)} %v_ref.1), custom_call_target="tpu_custom_call" | custom-call | flops 1073741824 | bytes 4194304 | tf_op jit(solution)/shard_map/pallas_call | solution.py:639
  49.5 1.3 %copy.8 = f32[16,2,16384]{2,1,0:T(2,128)} copy(f32[16,2,16384]{2,1,0:T(2,128)S(1)} %bitcast.9) | data formatting | bytes 4194304

commit v8 on v6

--- a/solution.py
+++ b/solution.py
@@ -392,6 +392,7 @@
 
     @pl.when(inner)
     def _():
+        signal(barrier, 1, mate)
         signal(barrier, 2, facing)
 
         def tell(i, carry):
@@ -404,16 +405,12 @@
             return carry
 
         lax.fori_loop(0, plane_dev, tell, 0)
-        signal(barrier, 1, mate)
         signal(barrier, plane_dev, first_cores_of_other_kind)
 
     @pl.when(outer)
     def _():
+        signal(barrier, 1, mate)
         signal(barrier, plane_dev - 1, other_second_cores)
-        signal(barrier, 1, mate)
-
-    for copy in keep + locals_:
-        copy.start()
 
     def send_facing():
         for k in range(chunks):
@@ -472,6 +469,8 @@
         for k in range(1, chunks):
             send(k, others, of_all)
 
+    for copy in keep + locals_:
+        copy.start()
     for copy in locals_:
         copy.wait()
     for w_copy, _ in gathers:

time: 51 us -> 51 us (level)
  no operation moved by 1% of the time
where the time goes in v8:
time: 51 us; the launch traced here: 50.8 us
  Pallas kernels  49.4 us (97%)
  local copies, waits for them, and re-layouts  1.32 us (3%)
    pallas_call x1, Pallas kernels, ladder(): pl.pallas_call(functools.partial(ladder_kernel, n_idx, n_slab), out_shape...  49.4 us
    unnamed x1, local copies, waits for them, and re-layouts  1.32 us

profile of v8, /device:TPU:15, one launch (start us, length us, event | category | flops | bytes accessed | tf_op | source)
XLA Modules:
  0.0 50.8 jit_solution(4303307215145557693)
XLA Ops:
  0.0 49.4 %shard_map.55 = f32[16,256,128]{2,1,0:T(8,128)S(1)} custom-call(bf16[16,128,2,128]{3,2,1,0:T(2,128)(2,1)} %bitcast.10, s32[512]{0:T(512)} %labels_ref.1, s32[2]{0:T(128)} %slab_labels_ref.1, s32[1,512]{1,0:T(1,128)} %bitcast.11, bf16[512,128]{1,0:T(8,128)(2,1)} %w_ref.1, bf16[8,32,128]{2,1,0:T(8,128)(2,1)} %v_ref.1), custom_call_target="tpu_custom_call" | custom-call | flops 1073741824 | bytes 4194304 | tf_op jit(solution)/shard_map/pallas_call | solution.py:638
  49.5 1.3 %copy.8 = f32[16,2,16384]{2,1,0:T(2,128)} copy(f32[16,2,16384]{2,1,0:T(2,128)S(1)} %bitcast.9) | data formatting | bytes 4194304

commit v9 on v6

--- a/solution.py
+++ b/solution.py
@@ -532,7 +532,7 @@
     def give(k, far):
         def body(j, carry):
             t = j % 2
-            q = j // 2 - 2 * t
+            q = j // 2 - 2 * t * (1 - flip(z // 2, far))
             right, up = q // 4, q // 2 % 2
             pe = (flip(z // 2, far) * 2 + t) * 2 + right + t * (up - right)
             ps = (up + t * (right - up)) * 2 + flip(core, q % 2)

time: 51 us -> 51 us (level)
  no operation moved by 1% of the time
where the time goes in v9:
time: 51 us; the launch traced here: 50.8 us
  Pallas kernels  49.5 us (97%)
  local copies, waits for them, and re-layouts  1.32 us (3%)
    pallas_call x1, Pallas kernels, ladder(): pl.pallas_call(functools.partial(ladder_kernel, n_idx, n_slab), out_shape...  49.5 us
    unnamed x1, local copies, waits for them, and re-layouts  1.32 us

profile of v9, /device:TPU:15, one launch (start us, length us, event | category | flops | bytes accessed | tf_op | source)
XLA Modules:
  0.0 50.8 jit_solution(15158595042846443425)
XLA Ops:
  0.0 49.5 %shard_map.55 = f32[16,256,128]{2,1,0:T(8,128)S(1)} custom-call(bf16[16,128,2,128]{3,2,1,0:T(2,128)(2,1)} %bitcast.10, s32[512]{0:T(512)} %labels_ref.1, s32[2]{0:T(128)} %slab_labels_ref.1, s32[1,512]{1,0:T(1,128)} %bitcast.11, bf16[512,128]{1,0:T(8,128)(2,1)} %w_ref.1, bf16[8,32,128]{2,1,0:T(8,128)(2,1)} %v_ref.1), custom_call_target="tpu_custom_call" | custom-call | flops 1073741824 | bytes 4194304 | tf_op jit(solution)/shard_map/pallas_call | solution.py:639
  49.5 1.3 %copy.8 = f32[16,2,16384]{2,1,0:T(2,128)} copy(f32[16,2,16384]{2,1,0:T(2,128)S(1)} %bitcast.9) | data formatting | bytes 4194304
